TPU v7x, 512 devices: a whole 4x4x16 slice. The times are simulated.
512 devices in a mesh: dp: 64 (over z, x), ctx: 8 (over y, core).
Axes of the slice: x: 4, y: 4, z: 16, core: 2. Of those that a mesh axis runs over, the one named last changes fastest.
Arguments:
- events: bfloat16 [64, 1024, 512], P('dp', 'ctx'), may hold values from -6 to 6
- keep: int32 [64, 1024], P('dp', 'ctx'), may hold values 0 or 1
- lengths: int32 [64], P('dp'), may hold values from 1 to 1024, as said below
- cotangent: bfloat16 [64, 1024, 512], P('dp', 'ctx'), may hold values from -6 to 6
- w_in: bfloat16 [512, 2048], replicated, may hold values from -0.25 to 0.25
- w_out: bfloat16 [512, 512], replicated, may hold values from -0.25 to 0.25
Outputs:
- output: bfloat16 [64, 1024, 512], P('dp', 'ctx')
- grad_events: bfloat16 [64, 1024, 512], P('dp', 'ctx')
- grad_w_out: float32 [512, 512], P('dp')
Inputs may be any that keep to these rules, and one draw needn't show every extreme that they name: `lengths`: some history has length exactly 1024.
All inputs are finite; a program needn't handle non-finite values. No bound on the sum of `keep` on one device may be relied on, other than what follows from the above.
Results may differ from a plain program's by a relative error of at most 0.0074.
Values may be sent and summed in bfloat16 or wider, within the bound.
A program may use at most 64 MiB of HBM per device.

v0:
```python
import functools
import math

import jax
import jax.numpy as jnp
from jax import lax
from jax.experimental import pallas as pl
from jax.experimental.pallas import tpu as pltpu
from jax.sharding import PartitionSpec as P

HEADS = 4
DH = 128
WIDTH = HEADS * DH
X_CHIPS = 4
EPSILON = 1e-06
MESH = pl.DeviceIdType.MESH
F32 = jnp.float32
BF16 = jnp.bfloat16
U_COL, V_COL, Q_COL, K_COL = 0, WIDTH, 2 * WIDTH, 3 * WIDTH


def silu_parts(v):
    s = 0.5 * jnp.tanh(0.5 * v) + 0.5
    a = v * s
    return a, s + a * (1.0 - s)


def mul(a, b):
    return jnp.dot(a, b, preferred_element_type=F32)


def mul_t(a, b):
    return lax.dot_general(a, b, (((1,), (1,)), ((), ())), preferred_element_type=F32)


class Ring:
    def __init__(self, buf, rows, n, pos, core, ssem, rsem, place):
        self.buf, self.rows, self.n, self.pos, self.core = buf, rows, n, pos, core
        self.ssem, self.rsem = ssem, rsem
        self.other = 1 - core
        self.sib = place(pos, self.other)
        self.right, self.left = place((pos + 1) % n, self.other), place((pos + n - 1) % n, self.other)
        self.l, self.r, self.f = (pos + n - 1) % n, (pos + 1) % n, (pos + 2) % n

    def copy(self, chip, core, first, count, k, sem, to):
        rows = self.rows // 4
        start = pl.multiple_of((chip * 2 + core) * self.rows + first * rows, rows)
        part = self.buf.at[pl.ds(start, count * rows)]
        return pltpu.make_async_remote_copy(
            src_ref=part, dst_ref=part, send_sem=self.ssem.at[k], recv_sem=self.rsem.at[sem],
            device_id=to, device_id_type=MESH,
        )

    def quarter(self, chip, core, q, k, to):
        return self.copy(chip, core, q, 1, k, chip * 4 + q, to)

    def hand(self, chip, core, half, k):
        return self.copy(chip, core, half * 2, 2, k, 4 * self.n + chip * 2 + half, self.sib)

    def first(self):
        near = []
        if self.n > 1:
            for n in range(2):
                near.append(self.quarter(self.pos, self.core, n, 2 + n, self.right))
                near.append(self.quarter(self.pos, self.core, n + 2, 6 + n, self.left))
        return near + [self.hand(self.pos, self.core, half, half) for half in range(2)]

    def second(self):
        near = []
        if self.n > 1:
            for n in range(2):
                near.append(self.quarter(self.pos, self.core, n + 2, 4 + n, self.right))
                near.append(self.quarter(self.pos, self.core, n, 8 + n, self.left))
        return near

    def passed(self):
        steps = []
        for n in range(2):
            steps.append((self.l, n, self.quarter(self.l, self.other, n, 10 + n, self.right)))
            steps.append((self.r, 2 + n, self.quarter(self.r, self.other, 2 + n, 12 + n, self.left)))
        return steps

    def wait(self, chip, core, first, count=1):
        for q in range(first, first + count):
            self.quarter(chip, core, q, 0, self.sib).wait_recv()

    def wait_handed(self, chip, core):
        for half in range(2):
            self.hand(chip, core, half, 0).wait_recv()

    def start(self, copies):
        for copy in copies:
            copy.start()

    def relay(self):
        for chip, q, copy in self.passed():
            self.wait(chip, self.other, q)
            copy.start()

    def hand_near(self):
        self.hand(self.l, self.other, 0, 14).start()
        self.hand(self.r, self.other, 1, 17).start()
        self.wait(self.l, self.other, 2, 2)
        self.hand(self.l, self.other, 1, 15).start()
        self.wait(self.r, self.other, 0, 2)
        self.hand(self.r, self.other, 0, 16).start()

    def hand_far(self):
        for half in range(2):
            self.wait(self.f, self.core, half * 2, 2)
            self.hand(self.f, self.core, half, 18 + half).start()

    def done(self):
        for copy in self.first() + self.second():
            copy.wait_send()
        if self.n > 1:
            for _, _, copy in self.passed():
                copy.wait_send()
            for n, chip in enumerate((self.l, self.r, self.f)):
                for half in range(2):
                    self.hand(chip, self.core if n == 2 else self.other, half, 14 + 2 * n + half).wait_send()


class Star:
    def __init__(self, buf, rows, n, pos, core, ssem, rsem, place):
        self.buf, self.rows, self.n, self.pos, self.core = buf, rows, n, pos, core
        self.ssem, self.rsem, self.place = ssem, rsem, place

    def copy(self, chip, core, k, sem, to):
        start = pl.multiple_of((chip * 2 + core) * self.rows, self.rows)
        part = self.buf.at[pl.ds(start, self.rows)]
        return pltpu.make_async_remote_copy(
            src_ref=part, dst_ref=part, send_sem=self.ssem.at[k], recv_sem=self.rsem.at[sem],
            device_id=to, device_id_type=MESH,
        )

    def out(self, d):
        return self.copy(self.pos, self.core, d, self.pos, self.place((self.pos + d) % self.n, self.core))

    def hand(self, d):
        chip = (self.pos + d) % self.n
        return self.copy(chip, self.core, self.n + d, self.n + chip, self.place(self.pos, 1 - self.core))

    def start(self):
        for d in range(1, self.n):
            self.out(d).start()
        self.hand(0).start()

    def hand_over(self):
        for d in range(1, self.n):
            chip = (self.pos + d) % self.n
            self.copy(chip, self.core, 0, chip, self.place(self.pos, self.core)).wait_recv()
            self.hand(d).start()

    def wait_other(self):
        for d in range(self.n):
            chip = (self.pos + d) % self.n
            self.copy(chip, 1 - self.core, 0, self.n + chip, self.place(self.pos, self.core)).wait_recv()

    def done(self):
        for d in range(1, self.n):
            self.out(d).wait_send()
        for d in range(self.n):
            self.hand(d).wait_send()


def kernel(
    Z, X, Y,
    events, keep, lengths, cotangent, w_in, w_out,
    out, grad_events, grad_w_out,
    keep_v, e_all, act_all, do_all, cot_all, w_in_v, w_out_v, slope_v, gg_v, gu_v, att_v, dq_v, dk_v, dv_v, ge_v,
    g_v, p_v, w_v, gt_send, gt_all, z_send, z_recv, c_recv,
    plane_sem, z_sem, local_sem, e_ssem, e_rsem, d_ssem, d_rsem, cot_ssem, cot_rsem, gt_ssem, gt_rsem, z_ssem, z_rsem, c_ssem, c_rsem,
):
    R = events.shape[0]
    D = events.shape[1]
    PAIR = 2 * R
    S = 2 * X
    ZH = Z // 2
    RD = D // (Z * X)
    scale = 1.0 / math.sqrt(DH)
    dp, ctx = lax.axis_index("dp"), lax.axis_index("ctx")
    z, x = dp // X, dp % X
    y, core = ctx // 2, ctx % 2
    other = 1 - core
    sib = y * 2 + other
    mine = x * 2 + core

    def block(b):
        return pl.ds(pl.multiple_of(b * R, R), R)

    def pair(c):
        return pl.ds(pl.multiple_of(c * PAIR, PAIR), PAIR)

    rows = block(ctx)

    ev_copy = pltpu.make_async_copy(events, e_all.at[rows], local_sem.at[0])
    ev_copy.start()
    keep_copy = pltpu.make_async_copy(keep, keep_v, local_sem.at[7])
    keep_copy.start()
    barrier = pltpu.get_barrier_semaphore()

    def greet(dp_to, ctx_to):
        pl.semaphore_signal(barrier, inc=1, device_id=(dp_to, ctx_to), device_id_type=MESH)

    for k in range(1, Y):
        greet(dp, ((y + k) % Y) * 2)
    for k in range(1, X):
        greet(z * X + (x + k) % X, y * 2)

    @pl.when(core == 1)
    def _():
        greet(dp, y * 2)

    cot_copy = pltpu.make_async_copy(cotangent, cot_all.at[block(mine)], local_sem.at[1])
    cot_copy.start()
    w_copies = []
    for g in range(4):
        cols = pl.ds(g * WIDTH, WIDTH)
        w_copies.append(pltpu.make_async_copy(w_in.at[:, cols], w_in_v.at[:, cols], local_sem.at[2 + g]))
    for copy in w_copies:
        copy.start()
    wo_copy = pltpu.make_async_copy(w_out, w_out_v, local_sem.at[6])
    wo_copy.start()

    ev_copy.wait()
    keep_copy.wait()
    lane = lax.broadcasted_iota(jnp.int32, (1, R), 1)
    live_row = jnp.where((keep_v[...] == 1) & (ctx * R + lane < lengths[0]), 1.0, 0.0)
    eye = lax.broadcasted_iota(jnp.int32, (R, R), 0) == lax.broadcasted_iota(jnp.int32, (R, R), 1)
    live = jnp.sum(jnp.where(eye, live_row, 0.0), axis=1, keepdims=True)
    e_all[rows, :] = (e_all[rows, :].astype(F32) * live).astype(BF16)

    @pl.when(core == 0)
    def _():
        pl.semaphore_wait(barrier, 2 * (Y - 1) + 2 * (X - 1) + 1)
        pl.semaphore_signal(plane_sem, inc=1, device_id=(dp, sib), device_id_type=MESH)

    @pl.when(core == 1)
    def _():
        pl.semaphore_wait(plane_sem, 1)


    def remote(buf, b, ssem, rsem, ctx_to):
        return pltpu.make_async_remote_copy(
            src_ref=buf.at[block(b)], dst_ref=buf.at[block(b)], send_sem=ssem, recv_sem=rsem.at[b],
            device_id=(dp, ctx_to), device_id_type=MESH,
        )

    def arrived(buf, b, ssem, rsem):
        remote(buf, b, ssem.at[0], rsem, sib).wait_recv()

    def each(low, high, body):
        def step(k, _):
            body(k)
            return _
        lax.fori_loop(low, high, step, 0)

    e_ring = Ring(e_all, R, Y, y, core, e_ssem, e_rsem, lambda chip, c: (dp, chip * 2 + c))
    c_star = Star(cot_all, R, X, x, core, cot_ssem, cot_rsem, lambda chip, c: (z * X + chip, y * 2 + c))
    e_ring.start(e_ring.first())

    @pl.when(core == z // ZH)
    def _():
        for k in range(1, Z):
            greet(((z + k) % Z) * X + x, y * 2 + 1)

    cot_copy.wait()

    own = e_all[rows, :]
    for g in range(4):
        w_copies[g].wait()
        for half in range(2):
            cols = pl.ds(g * WIDTH + half * 256, 256)
            a, slope = silu_parts(mul(own, w_in_v[:, cols]))
            act_all[rows, cols] = a.astype(BF16)
            slope_v[:, cols] = slope
    e_ring.start(e_ring.second())
    c_star.start()

    def project(b, *bases):
        for base in bases:
            for half in range(2):
                cols = pl.ds(base + half * 256, 256)
                a, _ = silu_parts(mul(e_all[block(b), :], w_in_v[:, cols]))
                act_all[block(b), cols] = a.astype(BF16)

    def head(base, h):
        return pl.ds(base + h * DH, DH)

    def allowed(query_major):
        first = lax.broadcasted_iota(jnp.int32, (R, PAIR), 0) + core * R
        second = lax.broadcasted_iota(jnp.int32, (R, PAIR), 1)
        return first >= second if query_major else second >= first

    def forward(c):
        for h in range(HEADS):
            s = mul_t(act_all[rows, head(Q_COL, h)], act_all[pair(c), head(K_COL, h)]) * scale
            a, slope = silu_parts(s)
            ok = allowed(True)
            g_v[c, h] = jnp.where(ok, slope * scale, 0.0)
            w_v[h] = jnp.where(ok, a, 0.0).astype(BF16)
        att_v[...] = jnp.concatenate([mul(w_v[h], act_all[pair(c), head(V_COL, h)]) for h in range(HEADS)], axis=1)

    def forward_block(c, k):
        cols = pl.ds(pl.multiple_of(k * R, R), R)
        keys = block(c * 2 + k)
        for h in range(HEADS):
            a, slope = silu_parts(mul_t(act_all[rows, head(Q_COL, h)], act_all[keys, head(K_COL, h)]) * scale)
            g_v[c, h, :, cols] = slope * scale
            w_v[h, :, pl.ds(0, R)] = a.astype(BF16)
        att_v[...] += jnp.concatenate(
            [mul(w_v[h, :, pl.ds(0, R)], act_all[keys, head(V_COL, h)]) for h in range(HEADS)], axis=1
        )

    def prepare(c):
        for h in range(HEADS):
            s = mul_t(act_all[rows, head(K_COL, h)], act_all[pair(c), head(Q_COL, h)]) * scale
            a, slope = silu_parts(s)
            ok = allowed(False)
            g_v[c + 1, h] = jnp.where(ok, slope * scale, 0.0)
            p_v[c, h] = jnp.where(ok, a, 0.0).astype(BF16)

    def prepare_block(c, k):
        cols = pl.ds(pl.multiple_of(k * R, R), R)
        for h in range(HEADS):
            s = mul_t(act_all[rows, head(K_COL, h)], act_all[block(c * 2 + k), head(Q_COL, h)]) * scale
            a, slope = silu_parts(s)
            g_v[c + 1, h, :, cols] = slope * scale
            p_v[c, h, :, cols] = a.astype(BF16)

    e_ring.wait_handed(y, other)
    project(sib, V_COL, Q_COL, K_COL)
    if Y > 1:
        e_ring.relay()
    forward(y)
    prepare(y)
    wo_copy.wait()
    gg_v[...] = mul_t(cot_all[block(mine), :], w_out_v[...])
    if Y > 1:
        e_ring.hand_near()

    def take(c, k):
        @pl.when(c < y)
        def _():
            project(c * 2 + k, V_COL, K_COL)
            forward_block(c, k)

        @pl.when(c > y)
        def _():
            project(c * 2 + k, Q_COL)
            prepare_block(c, k)

    def forward_two(c, d, k):
        one, two = block(c * 2 + k), block(d * 2 + k)
        cols = pl.ds(pl.multiple_of(k * R, R), R)
        both = jnp.concatenate([e_all[one, :], e_all[two, :]], axis=0)
        for base in (K_COL, V_COL):
            for half in range(2):
                at = pl.ds(base + half * 256, 256)
                a, _ = silu_parts(mul(both, w_in_v[:, at]))
                act_all[one, at] = a[:R].astype(BF16)
                act_all[two, at] = a[R:].astype(BF16)

        def pick(base, h):
            return jnp.concatenate([act_all[one, head(base, h)], act_all[two, head(base, h)]], axis=0)

        for h in range(HEADS):
            a, slope = silu_parts(mul_t(act_all[rows, head(Q_COL, h)], pick(K_COL, h)) * scale)
            g_v[c, h, :, cols] = slope[:, :R] * scale
            g_v[d, h, :, cols] = slope[:, R:] * scale
            w_v[h] = a.astype(BF16)
        att_v[...] += jnp.concatenate([mul(w_v[h], pick(V_COL, h)) for h in range(HEADS)], axis=1)

    def near_step(j):
        k = other + j * (core - other)

        @pl.when(j == 1)
        def _():
            e_ring.wait_handed(e_ring.r, k)
            e_ring.wait_handed(e_ring.l, k)

        @pl.when(y == Y - 1)
        def _():
            forward_two(e_ring.r, e_ring.l, k)

        @pl.when(y < Y - 1)
        def _():
            each(0, 2, lambda n: take((y + 1 + 2 * n) % Y, k))

    def far_step(j):
        k = core + j * (other - core)

        @pl.when(j == 1)
        def _():
            e_ring.wait_handed(e_ring.f, k)

        take(e_ring.f, k)

    if Y > 1:
        each(0, 2, near_step)
        e_ring.hand_far()
        each(0, 2, far_step)

    att = att_v[...]
    cen = att - jnp.mean(att, axis=1, keepdims=True)
    inv = lax.rsqrt(jnp.mean(cen * cen, axis=1, keepdims=True) + EPSILON)
    normed = cen * inv
    gate = act_all[rows, pl.ds(U_COL, WIDTH)].astype(F32)
    gated = normed * gate

    turned = jnp.transpose(gated).reshape(Z, X, RD, R)
    for to in range(X):
        gt_send[to] = turned[:, to].reshape(Z * RD, R).astype(BF16)

    def gt_part(s):
        return gt_all.at[:, block(s)]

    def gt_piece(c):
        return pl.ds(pl.multiple_of(c * (ZH * RD), ZH * RD), ZH * RD)

    def gt_out(d, swap):
        to = (x + d) % X
        c = other if swap else core
        return pltpu.make_async_remote_copy(
            src_ref=gt_send.at[to, gt_piece(c)], dst_ref=gt_part(mine),
            send_sem=gt_ssem.at[2 * d + swap], recv_sem=gt_rsem.at[mine],
            device_id=(z * X + to, y * 2 + c), device_id_type=MESH,
        )

    def gt_in(d, swap):
        source = ((x + d) % X) * 2 + (other if swap else core)
        return pltpu.make_async_remote_copy(
            src_ref=gt_send.at[x, gt_piece(core)], dst_ref=gt_part(source),
            send_sem=gt_ssem.at[2 * d + swap], recv_sem=gt_rsem.at[source],
            device_id=(dp, sib), device_id_type=MESH,
        )

    gt_order = [(d, swap) for d in sorted(range(1, X), key=lambda d: -min(d, X - d)) for swap in range(2)] + [(0, 1)]
    for d, swap in gt_order[:2]:
        gt_out(d, swap).start()
    gt_all[:, block(mine)] = gt_send[x, gt_piece(core), :]

    gg = gg_v[...]
    gn = gg * gate
    grad_att = (
        gn - jnp.mean(gn, axis=1, keepdims=True) - normed * jnp.mean(gn * normed, axis=1, keepdims=True)
    ) * inv * live
    do_all[rows, :] = grad_att.astype(BF16)
    for d, swap in gt_order[2:]:
        gt_out(d, swap).start()

    def d_out(c):
        return remote(do_all, ctx, d_ssem.at[c], d_rsem, c * 2 + core)

    d_sib = remote(do_all, ctx, d_ssem.at[y], d_rsem, sib)
    d_sib.start()
    each(0, y, lambda c: d_out(c).start())


    @pl.when(core == 1)
    def _():
        pl.semaphore_wait(barrier, Z - 1)
        pl.semaphore_signal(z_sem, inc=1, device_id=(dp, sib), device_id_type=MESH)

    c_star.hand_over()
    c_star.wait_other()
    for d, swap in gt_order:
        gt_in(d, swap).wait_recv()
    gram = mul(gt_all[...], cot_all[...]).reshape(ZH, RD, D)
    z_send[...] = jnp.concatenate([gram[:, :, : D // 2], gram[:, :, D // 2 :]], axis=1).astype(BF16)

    def z_out(k):
        return pltpu.make_async_remote_copy(
            src_ref=z_send.at[k], dst_ref=z_recv.at[z], send_sem=z_ssem.at[k], recv_sem=z_rsem.at[z],
            device_id=((core * ZH + k) * X + x, ctx), device_id_type=MESH,
        )

    def z_in(k):
        return pltpu.make_async_remote_copy(
            src_ref=z_send.at[0], dst_ref=z_recv.at[k], send_sem=z_ssem.at[0], recv_sem=z_rsem.at[k],
            device_id=(k * X + x, ctx), device_id_type=MESH,
        )

    def z_start(distances):
        for d in distances:
            to = (z + d) % Z

            @pl.when(to // ZH == core)
            def _():
                z_out(to % ZH).start()

    z_order = sorted(range(1, Z), key=lambda d: -min(d, Z - d))

    @pl.when(core == 0)
    def _():
        pl.semaphore_wait(z_sem, 1)

    z_start(z_order[:7])

    out[...] = mul(gated.astype(BF16), w_out_v[...]).astype(BF16)
    gu_v[...] = gg * normed
    z_start(z_order[7:9])

    dq_v[...] = jnp.zeros_like(dq_v)
    dk_v[...] = jnp.zeros_like(dk_v)
    dv_v[...] = jnp.zeros_like(dv_v)

    def query_step(c):
        for h in range(HEADS):
            gw = mul_t(do_all[rows, head(0, h)], act_all[pair(c), head(V_COL, h)])
            gs = (gw * g_v[c, h]).astype(BF16)
            dq_v[:, head(0, h)] += mul(gs, act_all[pair(c), head(K_COL, h)])

    each(0, y + 1, query_step)

    z_start(z_order[9:])

    def back(grad, base):
        cols = pl.ds(base, WIDTH)
        return mul_t((grad * slope_v[:, cols]).astype(BF16), w_in_v[:, cols])

    ge_v[...] = back(gu_v[...], U_COL) + back(dq_v[...], Q_COL)

    def key_step(c):
        for h in range(HEADS):
            do_h = do_all[pair(c), head(0, h)]
            gw = mul_t(act_all[rows, head(V_COL, h)], do_h)
            gs = (gw * g_v[c + 1, h]).astype(BF16)
            dv_v[:, head(0, h)] += mul(p_v[c, h], do_h)
            dk_v[:, head(0, h)] += mul(gs, act_all[pair(c), head(Q_COL, h)])

    arrived(do_all, sib, d_ssem, d_rsem)
    key_step(y)

    def hand_over(c):
        return remote(do_all, c * 2 + core, d_ssem.at[Y + c], d_rsem, sib)

    def later_chip(c):
        arrived(do_all, c * 2 + core, d_ssem, d_rsem)
        hand_over(c).start()
        arrived(do_all, c * 2 + other, d_ssem, d_rsem)
        key_step(c)

    each(y + 1, Y, later_chip)

    grad_events[...] = (ge_v[...] + back(dv_v[...], V_COL) + back(dk_v[...], K_COL)).astype(BF16)

    holder = z // ZH
    c_order = sorted(range(1, 2 * Y), key=lambda k: -min(k, 2 * Y - k))

    def c_out(k):
        return pltpu.make_async_remote_copy(
            src_ref=c_recv.at[y], dst_ref=c_recv.at[y], send_sem=c_ssem.at[k], recv_sem=c_rsem.at[y],
            device_id=(dp, (ctx + k) % (2 * Y)), device_id_type=MESH,
        )

    def c_in(k):
        return pltpu.make_async_remote_copy(
            src_ref=c_recv.at[k], dst_ref=c_recv.at[k], send_sem=c_ssem.at[0], recv_sem=c_rsem.at[k],
            device_id=(dp, sib), device_id_type=MESH,
        )

    e_ring.done()
    c_star.done()
    d_sib.wait_send()
    each(0, y, lambda c: d_out(c).wait_send())
    each(y + 1, Y, lambda c: hand_over(c).wait_send())
    for d, swap in gt_order:
        gt_out(d, swap).wait_send()

    def z_done(k):
        @pl.when(core * ZH + k != z)
        def _():
            z_out(k).wait_send()

    each(0, ZH, z_done)

    @pl.when(core == holder)
    def _():
        z_recv[z] = z_send[z % ZH]

        def wait_z(k):
            @pl.when(k != z)
            def _():
                z_in(k).wait_recv()

        each(0, Z, wait_z)
        total = jnp.sum(z_recv[...].astype(F32), axis=0)
        c_recv[y] = total.astype(BF16)
        for k in c_order:
            c_out(k).start()

    def wait_c(k):
        @pl.when(k * 2 + holder != ctx)
        def _():
            c_in(k).wait_recv()

    each(0, Y, wait_c)
    tokens = R * 2 * Y * Z * X
    total = jnp.sum(c_recv[...].astype(F32), axis=0) * (1.0 / math.sqrt(tokens))
    grad_w_out[...] = jnp.concatenate([total[:RD], total[RD:]], axis=1)

    @pl.when(core == holder)
    def _():
        each(1, 2 * Y, lambda k: c_out(k).wait_send())


def in_hbm(a):
    return pltpu.with_memory_space_constraint(a, pltpu.HBM)


def store(*refs):
    copies = [pltpu.make_async_copy(refs[n], refs[3 + n], refs[6].at[n]) for n in range(3)]
    for copy in copies:
        copy.start()
    for copy in copies:
        copy.wait()


def build(mesh, X):
    Z, Y = mesh.shape["dp"] // X, mesh.shape["ctx"] // 2

    def per_device(events, keep, lengths, cotangent, w_in, w_out):
        R, D = events.shape[1:]
        L = R * 2 * Y
        S = 2 * X
        ZH, RD = Z // 2, D // (Z * X)
        vmem = pl.BlockSpec(memory_space=pltpu.VMEM)
        hbm = pl.BlockSpec(memory_space=pltpu.HBM)
        dma = pltpu.SemaphoreType.DMA
        output, grad_events, grad_w_out = pl.pallas_call(
            functools.partial(kernel, Z, X, Y),
            out_shape=(pltpu.VMEM((R, D), BF16), pltpu.VMEM((R, D), BF16), pltpu.VMEM((RD, D), F32)),
            in_specs=[hbm, hbm, pl.BlockSpec(memory_space=pltpu.SMEM), hbm, hbm, hbm],
            out_specs=[vmem] * 3,
            scratch_shapes=[
                pltpu.VMEM((1, R), jnp.int32),
                pltpu.VMEM((L, D), BF16),
                pltpu.VMEM((L, 4 * WIDTH), BF16),
                pltpu.VMEM((L, WIDTH), BF16),
                pltpu.VMEM((S * R, D), BF16),
                pltpu.VMEM((D, 4 * WIDTH), BF16),
                pltpu.VMEM((WIDTH, D), BF16),
                pltpu.VMEM((R, 4 * WIDTH), F32),
                pltpu.VMEM((R, WIDTH), F32),
                pltpu.VMEM((R, WIDTH), F32),
                pltpu.VMEM((R, WIDTH), F32),
                pltpu.VMEM((R, WIDTH), F32),
                pltpu.VMEM((R, WIDTH), F32),
                pltpu.VMEM((R, WIDTH), F32),
                pltpu.VMEM((R, D), F32),
                pltpu.VMEM((Y + 1, HEADS, R, 2 * R), F32),
                pltpu.VMEM((Y, HEADS, R, 2 * R), BF16),
                pltpu.VMEM((HEADS, R, 2 * R), BF16),
                pltpu.VMEM((X, Z * RD, R), BF16),
                pltpu.VMEM((ZH * RD, S * R), BF16),
                pltpu.VMEM((ZH, 2 * RD, D // 2), BF16),
                pltpu.VMEM((Z, 2 * RD, D // 2), BF16),
                pltpu.VMEM((Y, 2 * RD, D // 2), BF16),
                pltpu.SemaphoreType.REGULAR, pltpu.SemaphoreType.REGULAR,
                dma((8,)),
                dma((20,)), dma((6 * Y,)),
                dma((2 * Y,)), dma((2 * Y,)),
                dma((2 * X,)), dma((2 * X,)),
                dma((S,)), dma((S,)),
                dma((ZH,)), dma((Z,)),
                dma((2 * Y,)), dma((Y,)),
            ],
            compiler_params=pltpu.CompilerParams(
                collective_id=0, has_side_effects=True, vmem_limit_bytes=56 * 1024 * 1024
            ),
            name="layer",
        )(in_hbm(events[0]), in_hbm(keep), lengths, in_hbm(cotangent[0]), in_hbm(w_in), in_hbm(w_out))
        output, grad_events, grad_w_out = pl.pallas_call(
            store,
            out_shape=(
                jax.ShapeDtypeStruct((R, D), BF16),
                jax.ShapeDtypeStruct((R, D), BF16),
                jax.ShapeDtypeStruct((RD, D), F32),
            ),
            in_specs=[vmem] * 3,
            out_specs=(hbm, hbm, hbm),
            scratch_shapes=[dma((3,))],
            name="store",
        )(*[pltpu.with_memory_space_constraint(a, pltpu.VMEM) for a in (output, grad_events, grad_w_out)])
        return (output[None], grad_events[None], grad_w_out)

    return jax.shard_map(
        per_device,
        mesh=mesh,
        in_specs=(P("dp", "ctx", None), P("dp", "ctx"), P("dp"), P("dp", "ctx", None), P(), P()),
        out_specs=(P("dp", "ctx", None), P("dp", "ctx", None), P("dp", None)),
        check_vma=False,
    )


def solution(mesh):
    return build(mesh, X_CHIPS)
```

profile of v0, /device:TPU:1, one launch (start us, length us, event | category | flops | bytes accessed | tf_op | source)
XLA Modules:
  0.0 43.1 jit_solution(15339058185154243598)
XLA Ops:
  1.3 41.1 %layer.1 = (bf16[128,512]{1,0:T(8,128)(2,1)S(1)}, bf16[128,512]{1,0:T(8,128)(2,1)S(1)}, f32[8,512]{1,0:T(8,128)S(1)}) custom-call(bf16[128,512]{1,0:T(8,128)(2,1)} %bitcast.4, s32[1,128]{1,0:T(1,128)} %keep.1, s32[1]{0:T(128)S(6)} %copy.9.lengths, bf16[128,512]{1,0:T(8,128)(2,1)} %bitcast.5, bf16[512,2048]{1,0:T(8,128)(2,1)} %w_in.1, bf16[512,512]{1,0:T(8,128)(2,1)} %w_out.1), custom_call_target="tpu_custom_call" | custom-call | tf_op jit(solution)/shard_map/layer/pallas_call | solution.py:632
  42.3 0.7 %store.1 = (bf16[128,512]{1,0:T(8,128)(2,1)}, bf16[128,512]{1,0:T(8,128)(2,1)}, f32[8,512]{1,0:T(8,128)}) custom-call(bf16[128,512]{1,0:T(8,128)(2,1)S(1)} %get-tuple-element.9.refs_0_, bf16[128,512]{1,0:T(8,128)(2,1)S(1)} %get-tuple-element.10.refs_1_, f32[8,512]{1,0:T(8,128)S(1)} %get-tuple-element.11.refs_2_), custom_call_target="tpu_custom_call" | custom-call | tf_op jit(solution)/shard_map/store/pallas_call | solution.py:675
where the time goes:
time: 43.2 us; the launch traced here: 43.1 us
  Pallas kernels  41.8 us (97%)
  between operations  1.28 us (3%)
    pallas_call x1, Pallas kernels, per_device(): pl.pallas_call(functools.partial(kernel, Z, X, Y), out_shape=(pltpu.VMEM(...  41.1 us

commit v1 on v0

--- a/solution.py
+++ b/solution.py
@@ -196,8 +196,6 @@
 
     ev_copy = pltpu.make_async_copy(events, e_all.at[rows], local_sem.at[0])
     ev_copy.start()
-    keep_copy = pltpu.make_async_copy(keep, keep_v, local_sem.at[7])
-    keep_copy.start()
     barrier = pltpu.get_barrier_semaphore()
 
     def greet(dp_to, ctx_to):
@@ -212,6 +210,8 @@
     def _():
         greet(dp, y * 2)
 
+    keep_copy = pltpu.make_async_copy(keep, keep_v, local_sem.at[7])
+    keep_copy.start()
     cot_copy = pltpu.make_async_copy(cotangent, cot_all.at[block(mine)], local_sem.at[1])
     cot_copy.start()
     w_copies = []
@@ -437,7 +437,7 @@
         )
 
     gt_order = [(d, swap) for d in sorted(range(1, X), key=lambda d: -min(d, X - d)) for swap in range(2)] + [(0, 1)]
-    for d, swap in gt_order[:2]:
+    for d, swap in gt_order:
         gt_out(d, swap).start()
     gt_all[:, block(mine)] = gt_send[x, gt_piece(core), :]
 
@@ -447,8 +447,6 @@
         gn - jnp.mean(gn, axis=1, keepdims=True) - normed * jnp.mean(gn * normed, axis=1, keepdims=True)
     ) * inv * live
     do_all[rows, :] = grad_att.astype(BF16)
-    for d, swap in gt_order[2:]:
-        gt_out(d, swap).start()
 
     def d_out(c):
         return remote(do_all, ctx, d_ssem.at[c], d_rsem, c * 2 + core)

time: 43.2 us -> 43 us (level)
  no operation moved by 1% of the time
where the time goes in v1:
time: 43 us; the launch traced here: 42.8 us
  Pallas kernels  41.6 us (97%)
  between operations  1.28 us (3%)
    pallas_call x1, Pallas kernels, per_device(): pl.pallas_call(functools.partial(kernel, Z, X, Y), out_shape=(pltpu.VMEM(...  40.8 us

profile of v1, /device:TPU:1, one launch (start us, length us, event | category | flops | bytes accessed | tf_op | source)
XLA Modules:
  0.0 42.8 jit_solution(15295503533392577552)
XLA Ops:
  1.3 40.8 %layer.1 = (bf16[128,512]{1,0:T(8,128)(2,1)S(1)}, bf16[128,512]{1,0:T(8,128)(2,1)S(1)}, f32[8,512]{1,0:T(8,128)S(1)}) custom-call(bf16[128,512]{1,0:T(8,128)(2,1)} %bitcast.4, s32[1,128]{1,0:T(1,128)} %keep.1, s32[1]{0:T(128)S(6)} %copy.9.lengths, bf16[128,512]{1,0:T(8,128)(2,1)} %bitcast.5, bf16[512,2048]{1,0:T(8,128)(2,1)} %w_in.1, bf16[512,512]{1,0:T(8,128)(2,1)} %w_out.1), custom_call_target="tpu_custom_call" | custom-call | tf_op jit(solution)/shard_map/layer/pallas_call | solution.py:630
  42.1 0.7 %store.1 = (bf16[128,512]{1,0:T(8,128)(2,1)}, bf16[128,512]{1,0:T(8,128)(2,1)}, f32[8,512]{1,0:T(8,128)}) custom-call(bf16[128,512]{1,0:T(8,128)(2,1)S(1)} %get-tuple-element.9.refs_0_, bf16[128,512]{1,0:T(8,128)(2,1)S(1)} %get-tuple-element.10.refs_1_, f32[8,512]{1,0:T(8,128)S(1)} %get-tuple-element.11.refs_2_), custom_call_target="tpu_custom_call" | custom-call | tf_op jit(solution)/shard_map/store/pallas_call | solution.py:673
